TPU v7x, 32 devices: a whole 2x2x4 slice. The times are simulated.
32 devices in a mesh: groups: 2 (over y), adapter: 4 (over z), tensor: 2 (over x), dp: 2 (over core).
Axes of the slice: x: 2, y: 2, z: 4, core: 2. Of those that a mesh axis runs over, the one named last changes fastest.
Arguments:
- tokens: bfloat16 [4096, 8192], P(('groups', 'adapter', 'dp'), 'tensor'), parts along dimension 0, may hold values from -6 to 6
- frozen_value_weight: bfloat16 [8192, 1024], P('tensor'), may hold values from -0.0625 to 0.0625
- adapter_down_weight: bfloat16 [128, 16, 8192], P(('groups', 'adapter'), None, 'tensor'), parts along dimension 0, may hold values from -0.0625 to 0.0625
- adapter_up_weight: bfloat16 [128, 16, 1024], P(('groups', 'adapter'), None, 'tensor'), parts along dimension 0, may hold values from -0.1875 to 0.1875
- token_adapter: int32 [4096], P(('groups', 'adapter', 'dp')), parts along dimension 0, may hold values from 0 to 63, as said below
- adapter_storage_row: int32 [128], P('groups'), parts along dimension 0, may hold values from 0 to 63, as said below
- upstream: bfloat16 [4096, 1024], P(('groups', 'adapter', 'dp'), 'tensor'), parts along dimension 0, may hold values from -6 to 6
Outputs:
- projected: bfloat16 [4096, 1024], P(('groups', 'adapter', 'dp'), 'tensor'), parts along dimension 0
- token_input_gradient: bfloat16 [4096, 8192], P(('groups', 'adapter', 'dp'), 'tensor'), parts along dimension 0
- grad_down: float32 [128, 16, 8192], P(('groups', 'adapter'), None, 'tensor'), parts along dimension 0
- grad_up: float32 [128, 16, 1024], P(('groups', 'adapter'), None, 'tensor'), parts along dimension 0
There are 2 independent parts, one for each index of `groups`. A program takes and returns all parts, laid end to end along the dimension named above; an argument that names none is the same for every part. Nothing has to cross between parts.
Inputs may be any that keep to these rules, and one draw needn't show every extreme that they name: A token's adapter is owned by index adapter_storage_row[token_adapter] // 16 of adapter. Of the 256 tokens of one device (aligned blocks of the token dimension), exactly 192 belong to one owner, the same owner for every device of one part; every other owner gets at most 22 of them, and some owner exactly 22. `adapter_storage_row`: A permutation.
All inputs are finite; a program needn't handle non-finite values.
Results may differ from a plain program's by a relative error of at most 0.0034.
Values may be sent and summed in bfloat16 or wider, within the bound.
A program may use at most 128 MiB of HBM per device.

v0:
```python
import jax
import jax.numpy as jnp
from jax import lax
from jax.sharding import PartitionSpec as P

adapter_scale = 2.0


def route_table(token_adapter, adapter_storage_row, each_holder, holder_list):
    matches = (
        token_adapter[:, None] == jnp.arange(adapter_storage_row.shape[0], dtype=jnp.int32)[None, :]
    )
    storage = jnp.sum(jnp.where(matches, adapter_storage_row[None, :], 0), axis=1)
    owner_of = storage // each_holder
    local_slot = storage % each_holder
    owner_hits = (owner_of[:, None] == jnp.arange(holder_list, dtype=jnp.int32)[None, :]).astype(
        jnp.int32
    )
    before = jnp.cumsum(owner_hits, axis=0) - owner_hits
    position = jnp.sum(before * owner_hits, axis=1)
    loads = jnp.sum(owner_hits, axis=0)
    return (owner_of, local_slot, position, loads)


def pack_rows(rows, target, buffer_rows):
    return jnp.zeros((buffer_rows,) + rows.shape[1:], rows.dtype).at[target].set(rows, mode="drop")


def spread(choice_mask, values):
    return choice_mask[:, :, None] * values[:, None, :]


def rank_partial_sum(features, choice_mask, down_matrix):
    every = jnp.einsum("md,erd->mer", features, down_matrix, preferred_element_type=jnp.float32)
    return jnp.sum(every * choice_mask[:, :, None].astype(jnp.float32), axis=1)


def backward_partial_sum(upper, choice_mask, up_matrix):
    every = jnp.einsum("mk,erk->mer", upper, up_matrix, preferred_element_type=jnp.float32)
    return jnp.sum(every * choice_mask[:, :, None].astype(jnp.float32), axis=1)


def adapter_value_rows(choice_mask, rank_cast, up_matrix):
    return (
        adapter_scale
        * jnp.einsum(
            "mer,erk->mk",
            spread(choice_mask, rank_cast),
            up_matrix,
            preferred_element_type=jnp.float32,
        )
    ).astype(jnp.bfloat16)


def adapter_input(choice_mask, backward_cast, down_matrix):
    return (
        adapter_scale
        * jnp.einsum(
            "mer,erd->md",
            spread(choice_mask, backward_cast),
            down_matrix,
            preferred_element_type=jnp.float32,
        )
    ).astype(jnp.bfloat16)


def adapter_grads(choice_mask, rank_cast, backward_cast, features, upper):
    down_piece = adapter_scale * jnp.einsum(
        "mer,md->erd",
        spread(choice_mask, backward_cast),
        features,
        preferred_element_type=jnp.float32,
    )
    up_piece = adapter_scale * jnp.einsum(
        "mer,mk->erk", spread(choice_mask, rank_cast), upper, preferred_element_type=jnp.float32
    )
    return (down_piece, up_piece)


def shards(
    tokens,
    frozen_value_weight,
    adapter_down_weight,
    adapter_up_weight,
    token_adapter,
    adapter_storage_row,
    upstream,
):
    holder_list = lax.axis_size("adapter")
    each_holder = adapter_down_weight.shape[0]
    tok_dev = tokens.shape[0]
    slot_capacity = 3 * tok_dev // holder_list
    owner_of, local_slot, position, loads = route_table(
        token_adapter, adapter_storage_row, each_holder, holder_list
    )
    slot_range = jnp.arange(each_holder, dtype=jnp.int32)
    base_part = jnp.dot(tokens, frozen_value_weight, preferred_element_type=jnp.float32)
    target = owner_of * slot_capacity + position
    buffer_rows = holder_list * slot_capacity
    pick = jnp.minimum(target, buffer_rows - 1)
    feature_send = pack_rows(tokens, target, buffer_rows).reshape(holder_list, slot_capacity, -1)
    slot_send = (
        jnp.full((buffer_rows,), each_holder, jnp.int32)
        .at[target]
        .set(local_slot, mode="drop")
        .reshape(holder_list, slot_capacity)
    )
    upstream_send = pack_rows(upstream, target, buffer_rows).reshape(holder_list, slot_capacity, -1)
    received_features, recv_slots = (
        lax.all_to_all(feature_send, "adapter", split_axis=0, concat_axis=0, tiled=True),
        lax.all_to_all(slot_send, "adapter", split_axis=0, concat_axis=0, tiled=True),
    )
    received_features = received_features.reshape(buffer_rows, -1)
    recv_slots = recv_slots.reshape(buffer_rows)
    choice_mask = (recv_slots[:, None] == slot_range[None, :]).astype(jnp.bfloat16)
    rank_piece = rank_partial_sum(received_features, choice_mask, adapter_down_weight)
    low_all = rank_piece
    low_all = lax.psum(low_all, "tensor")
    rank_cast = low_all.astype(jnp.bfloat16)
    adapter_row_block = adapter_value_rows(choice_mask, rank_cast, adapter_up_weight).reshape(
        holder_list, slot_capacity, -1
    )
    adapter_held_here = lax.all_to_all(
        adapter_row_block, "adapter", split_axis=0, concat_axis=0, tiled=True
    ).reshape(buffer_rows, -1)[pick]
    frozen_portion = lax.psum_scatter(base_part, "tensor", scatter_dimension=1, tiled=True)
    projected = (frozen_portion + adapter_held_here.astype(jnp.float32)).astype(jnp.bfloat16)
    frozen_backward = lax.dot_general(
        lax.all_gather(upstream, "tensor", axis=1, tiled=True),
        frozen_value_weight,
        (((1,), (1,)), ((), ())),
        preferred_element_type=jnp.float32,
    )
    received_incoming_gradient = lax.all_to_all(
        upstream_send, "adapter", split_axis=0, concat_axis=0, tiled=True
    )
    received_incoming_gradient = received_incoming_gradient.reshape(buffer_rows, -1)
    backward_piece = backward_partial_sum(
        received_incoming_gradient, choice_mask, adapter_up_weight
    )
    back_all = backward_piece
    back_all = lax.psum(back_all, "tensor")
    backward_cast = back_all.astype(jnp.bfloat16)
    down_local, up_local = adapter_grads(
        choice_mask, rank_cast, backward_cast, received_features, received_incoming_gradient
    )
    token_input_rows = adapter_input(choice_mask, backward_cast, adapter_down_weight).reshape(
        holder_list, slot_capacity, -1
    )
    input_mine = lax.all_to_all(
        token_input_rows, "adapter", split_axis=0, concat_axis=0, tiled=True
    ).reshape(buffer_rows, -1)[pick]
    down_gradient_sum, up_gradient_sum = lax.psum((down_local, up_local), "dp")
    token_input_gradient = (frozen_backward + input_mine.astype(jnp.float32)).astype(jnp.bfloat16)
    return (projected, token_input_gradient, down_gradient_sum, up_gradient_sum)


def solution(mesh):
    return jax.shard_map(
        shards,
        mesh=mesh,
        in_specs=(
            P(("groups", "adapter", "dp"), "tensor"),
            P("tensor", None),
            P(("groups", "adapter"), None, "tensor"),
            P(("groups", "adapter"), None, "tensor"),
            P(("groups", "adapter", "dp")),
            P("groups"),
            P(("groups", "adapter", "dp"), "tensor"),
        ),
        out_specs=(
            P(("groups", "adapter", "dp"), "tensor"),
            P(("groups", "adapter", "dp"), "tensor"),
            P(("groups", "adapter"), None, "tensor"),
            P(("groups", "adapter"), None, "tensor"),
        ),
        check_vma=False,
    )
```

profile of v0, /device:TPU:0, one launch (start us, length us, event | category | flops | bytes accessed | tf_op | source)
XLA Modules:
  0.0 397.2 jit_solution(18295719762680251807)
XLA Ops:
  12.7 6.3 %all-to-all-start = ((s32[4,1,192]{2,1,0:T(1,128)}), s32[4,1,192]{2,1,0:T(1,128)S(1)}, u32[]{:S(2)}, u32[]{:S(2)}) async-start(s32[4,1,192]{2,1,0:T(1,128)} %all_to_all.18), calls=%async_computation.1 | async-start | bytes 8192 | tf_op jit(solution)/shard_map/all_to_all | solution.py:111
  19.1 2.9 scatter_custom_fusion.2
  21.9 2.7 all-to-all-done
  24.6 3.5 all-to-all-start.3
  28.1 8.2 %scatter_custom_fusion.1 = bf16[768,4096]{1,0:T(8,128)(2,1)} fusion(s32[256]{0:T(256)S(1)} %bitcast.75, bf16[256,4096]{1,0:T(8,128)(2,1)} %param.7, bf16[]{:T(256)} %constant.47.clone.1), kind=kCustom, calls=%fused_computation.10 | custom fusion | bytes 6291968 | tf_op jit(solution)/shard_map/scatter | solution.py:26
  36.4 10.7 %all-to-all-done.3 = bf16[4,192,512]{2,1,0:T(8,128)(2,1)S(1)} async-done(((bf16[4,192,512]{2,1,0:T(8,128)(2,1)}), bf16[4,192,512]{2,1,0:T(8,128)(2,1)S(1)}, u32[]{:S(2)}, u32[]{:S(2)}) %all-to-all-start.3) | async-done | bytes 786464 | tf_op jit(solution)/shard_map/all_to_all | solution.py:134
  47.1 5.4 %all-to-all-start.1 = ((bf16[4,192,4096]{2,1,0:T(8,128)(2,1)}), bf16[4,192,4096]{2,1,0:T(8,128)(2,1)}, u32[]{:S(2)}, u32[]{:S(2)}) async-start(bf16[4,192,4096]{2,1,0:T(8,128)(2,1)} %bitcast.63), calls=%async_computation.2 | async-start | bytes 12582912 | tf_op jit(solution)/shard_map/all_to_all | solution.py:110
  53.0 137.1 %all-to-all-done.1 = bf16[4,192,4096]{2,1,0:T(8,128)(2,1)} async-done(((bf16[4,192,4096]{2,1,0:T(8,128)(2,1)}), bf16[4,192,4096]{2,1,0:T(8,128)(2,1)}, u32[]{:S(2)}, u32[]{:S(2)}) %all-to-all-start.1) | async-done | bytes 6291488 | tf_op jit(solution)/shard_map/all_to_all | solution.py:110
  190.1 4.6 %fusion.6 = f32[768,16]{0,1:T(8,128)S(1)} fusion(bf16[768,4096,1]{1,0,2:T(8,128)(2,1)} %bitcast.8, bf16[16,16,4096]{2,1,0:T(8,128)(2,1)S(1)} %copy-done, f32[768,16]{0,1:T(8,128)S(1)} %get-tuple-element.11), kind=kOutput, calls=%fused_computation.18 | convolution fusion | flops 1610993664 | bytes 8486912 | tf_op jit(solution)/shard_map/md,erd->mer/dot_general | solution.py:34
  194.7 9.6 %all-reduce.1 = (bf16[768,16]{0,1:T(8,128)(2,1)S(1)}, bf16[768,16]{0,1:T(8,128)(2,1)S(1)}) all-reduce(f32[768,16]{0,1:T(8,128)S(1)} %fusion.6, f32[768,16]{0,1:T(8,128)S(1)} %fusion.5), channel_id=1, replica_groups=mesh['groups'=2,'adapter'=4,'tensor'=2,'dp'=2] {'tensor'}, use_global_device_ids=true, to_apply=%region_8.9 | all-reduce | flops 24576 | bytes 147456 | tf_op jit(solution)/shard_map/psum | solution.py:118
  205.6 3.7 all-to-all-start.2
  209.3 4.5 %fusion = bf16[768,4096]{1,0:T(8,128)(2,1)} fusion(bf16[16,16,4096]{2,1,0:T(8,128)(2,1)S(1)} %copy-done, bf16[768,16]{0,1:T(8,128)(2,1)S(1)} %get-tuple-element.7, bf16[768,16]{0,1:T(8,128)(2,1)S(1)} %get-tuple-element.10), kind=kOutput, calls=%fused_computation.6 | convolution fusion | flops 1617100800 | bytes 8437760 | tf_op jit(solution)/shard_map/mer,erd->md/dot_general | solution.py:58
  213.8 12.5 %all-to-all-done.2 = bf16[4,192,512]{2,1,0:T(8,128)(2,1)S(1)} async-done(((bf16[4,192,512]{2,1,0:T(8,128)(2,1)}), bf16[4,192,512]{2,1,0:T(8,128)(2,1)S(1)}, u32[]{:S(2)}, u32[]{:S(2)}) %all-to-all-start.2) | async-done | bytes 786464 | tf_op jit(solution)/shard_map/all_to_all | solution.py:123
  226.3 5.2 %all-to-all-start.4 = ((bf16[4,192,4096]{2,1,0:T(8,128)(2,1)}), bf16[4,192,4096]{2,1,0:T(8,128)(2,1)}, u32[]{:S(2)}, u32[]{:S(2)}) async-start(bf16[4,192,4096]{2,1,0:T(8,128)(2,1)} %bitcast.65), calls=%async_computation.5 | async-start | bytes 12582912 | tf_op jit(solution)/shard_map/all_to_all | solution.py:150
  231.6 7.3 %fusion.28 = f32[256,1024]{1,0:T(8,128)} fusion(bf16[256,4096]{1,0:T(8,128)(2,1)} %param.7, bf16[4096,1024]{1,0:T(8,128)(2,1)} %param.8), kind=kOutput, calls=%fused_computation.68 | convolution fusion | flops 2147483648 | bytes 11534336 | tf_op jit(solution)/shard_map/dot_general | solution.py:97
  239.0 2.3 convolution_multiply_fusion.3
  241.3 6.6 %convolution_multiply_fusion = f32[16,16,4096]{2,1,0:T(8,128)} fusion(bf16[768,4096,1]{1,0,2:T(8,128)(2,1)} %bitcast.8, bf16[768,16]{0,1:T(8,128)(2,1)S(1)} %get-tuple-element.7, bf16[768,16]{0,1:T(8,128)(2,1)S(1)} %get-tuple-element.10), kind=kOutput, calls=%fused_computation.7 | convolution fusion | flops 1611857920 | bytes 10534912 | tf_op jit(solution)/shard_map/mer,md->erd/dot_general | solution.py:68
  248.9 14.6 %all_gather.3 = bf16[256,1024]{1,0:T(8,128)(2,1)} all-gather(bf16[256,512]{1,0:T(8,128)(2,1)S(1)} %copy-done.4), channel_id=1, replica_groups=mesh['groups'=2,'adapter'=4,'tensor'=2,'dp'=2] {'tensor'}, dimensions={1}, use_global_device_ids=true | all-gather | bytes 786432 | tf_op jit(solution)/shard_map/all_gather | solution.py:129
  264.7 1.4 reduce-scatter.2.cloned.1.call-done
  266.1 1.8 add_convert_fusion
  267.9 99.8 %all-to-all-done.4 = bf16[4,192,4096]{2,1,0:T(8,128)(2,1)} async-done(((bf16[4,192,4096]{2,1,0:T(8,128)(2,1)}), bf16[4,192,4096]{2,1,0:T(8,128)(2,1)}, u32[]{:S(2)}, u32[]{:S(2)}) %all-to-all-start.4) | async-done | bytes 6291488 | tf_op jit(solution)/shard_map/all_to_all | solution.py:150
  367.7 8.9 %gather_fusion.1 = bf16[256,4096]{1,0:T(8,128)(2,1)} fusion(bf16[768,4096]{1,0:T(8,128)(2,1)} %bitcast.18, s32[1024]{0:T(1024)S(1)} %pad_clamp_fusion), kind=kCustom, calls=%fused_computation.1 | custom fusion | bytes 4195328 | tf_op jit(solution)/shard_map/gather | solution.py:150
  376.6 7.7 %fusion.1 = bf16[256,4096]{1,0:T(8,128)(2,1)} fusion(bf16[256,1024]{1,0:T(8,128)(2,1)S(1)} %copy-done.2, bf16[4096,1024]{1,0:T(8,128)(2,1)} %param.8, bf16[256,4096]{1,0:T(8,128)(2,1)} %gather_fusion.1), kind=kOutput, calls=%fused_computation.9 | convolution fusion | flops 2150629376 | bytes 13107200 | tf_op jit(solution)/shard_map/dot_general | solution.py:128
  384.3 4.7 %copy.21 = f32[16,16,4096]{2,1,0:T(8,128)} copy(f32[16,16,4096]{2,1,0:T(8,128)} %get-tuple-element.16) | data formatting | bytes 8388608
  (41 shorter events, 9.5 us)
Async XLA Ops:
  8.0 182.1 %copy-start = (bf16[16,16,4096]{2,1,0:T(8,128)(2,1)S(1)}, bf16[16,16,4096]{2,1,0:T(8,128)(2,1)}, u32[]{:S(2)}) copy-start(bf16[16,16,4096]{2,1,0:T(8,128)(2,1)} %param.9) | copy-start | bytes 6291460
  12.7 11.9 %all-to-all-start = ((s32[4,1,192]{2,1,0:T(1,128)}), s32[4,1,192]{2,1,0:T(1,128)S(1)}, u32[]{:S(2)}, u32[]{:S(2)}) async-start(s32[4,1,192]{2,1,0:T(1,128)} %all_to_all.18), calls=%async_computation.1 | async-start | bytes 8192 | tf_op jit(solution)/shard_map/all_to_all | solution.py:111
  24.6 22.4 %all-to-all-start.3 = ((bf16[4,192,512]{2,1,0:T(8,128)(2,1)}), bf16[4,192,512]{2,1,0:T(8,128)(2,1)S(1)}, u32[]{:S(2)}, u32[]{:S(2)}) async-start(bf16[4,192,512]{2,1,0:T(8,128)(2,1)} %bitcast.13), calls=%async_computation.4 | async-start | bytes 1572864 | tf_op jit(solution)/shard_map/all_to_all | solution.py:134
  47.1 5.5 %copy-start.1 = (bf16[4,192,512]{2,1,0:T(8,128)(2,1)}, bf16[4,192,512]{2,1,0:T(8,128)(2,1)S(1)}, u32[]{:S(2)}) copy-start(bf16[4,192,512]{2,1,0:T(8,128)(2,1)S(1)} %all-to-all-done.3) | copy-start | bytes 2359300
  47.1 5.6 %copy-start.5 = (bf16[16,16,512]{2,1,0:T(8,128)(2,1)S(1)}, bf16[16,16,512]{2,1,0:T(8,128)(2,1)}, u32[]{:S(2)}) copy-start(bf16[16,16,512]{2,1,0:T(8,128)(2,1)} %param.10) | copy-start | bytes 786436
  47.1 143.1 %all-to-all-start.1 = ((bf16[4,192,4096]{2,1,0:T(8,128)(2,1)}), bf16[4,192,4096]{2,1,0:T(8,128)(2,1)}, u32[]{:S(2)}, u32[]{:S(2)}) async-start(bf16[4,192,4096]{2,1,0:T(8,128)(2,1)} %bitcast.63), calls=%async_computation.2 | async-start | bytes 12582912 | tf_op jit(solution)/shard_map/all_to_all | solution.py:110
  205.6 20.7 %all-to-all-start.2 = ((bf16[4,192,512]{2,1,0:T(8,128)(2,1)}), bf16[4,192,512]{2,1,0:T(8,128)(2,1)S(1)}, u32[]{:S(2)}, u32[]{:S(2)}) async-start(bf16[4,192,512]{2,1,0:T(8,128)(2,1)} %bitcast.68), calls=%async_computation.3 | async-start | bytes 1572864 | tf_op jit(solution)/shard_map/all_to_all | solution.py:123
  226.3 141.4 %all-to-all-start.4 = ((bf16[4,192,4096]{2,1,0:T(8,128)(2,1)}), bf16[4,192,4096]{2,1,0:T(8,128)(2,1)}, u32[]{:S(2)}, u32[]{:S(2)}) async-start(bf16[4,192,4096]{2,1,0:T(8,128)(2,1)} %bitcast.65), calls=%async_computation.5 | async-start | bytes 12582912 | tf_op jit(solution)/shard_map/all_to_all | solution.py:150
  231.6 34.5 %reduce-scatter.2.cloned.1.call-start = ((), (), s32[]{:S(2)}) async-start(), calls=%async_computation.6 | async-start | bytes 1572864 | tf_op jit(solution)/shard_map/reduce_scatter | solution.py:126
  239.0 145.3 %all-reduce.4.cloned.1.call-start = ((), (), s32[]{:S(2)}) async-start(), calls=%async_computation.7 | async-start | bytes 9437184 | tf_op jit(solution)/shard_map/psum | solution.py:153
  248.0 0.9 copy-start.4
  367.7 8.9 %copy-start.2 = (bf16[256,1024]{1,0:T(8,128)(2,1)S(1)}, bf16[256,1024]{1,0:T(8,128)(2,1)}, u32[]{:S(2)}) copy-start(bf16[256,1024]{1,0:T(8,128)(2,1)} %all_gather.3) | copy-start | bytes 1572868
  384.3 4.7 %copy-start.3 = (f32[16,16,512]{2,1,0:T(8,128)S(1)}, f32[16,16,512]{2,1,0:T(8,128)}, u32[]{:S(2)}) copy-start(f32[16,16,512]{2,1,0:T(8,128)} %get-tuple-element.17) | copy-start | bytes 1572868
Sparse Core Ops, SparseCore 0:
  239.1 26.9 reduce-scatter.1
Sparse Core Ops, SparseCore 1:
  248.1 29.7 all-reduce.3
where the time goes:
time: 398 us; the launch traced here: 397 us
  waiting for transfers between devices  264 us (66%)
  matrix products  34.7 us (9%)
  local copies, waits for them, and re-layouts  30 us (8%)
  starting transfers between devices  24.2 us (6%)
  blocking collectives  24.2 us (6%)
  between operations  15.6 us (4%)
  other arithmetic  4.19 us (1%)
    all_to_all x1, waiting for transfers between devices, shards(): lax.all_to_all(feature_send, 'adapter', split_axis=0, concat_axis=0, tile...  137 us
    all_to_all x1, waiting for transfers between devices, shards(): lax.all_to_all(token_input_rows, 'adapter', split_axis=0, concat_axis=0,...  99.8 us
    all_gather x1, blocking collectives, shards(): lax.all_gather(upstream, 'tensor', axis=1, tiled=True)  14.6 us
    all_to_all x1, waiting for transfers between devices, shards(): lax.all_to_all(adapter_row_block, 'adapter', split_axis=0, concat_axis=0,...  12.5 us
    scatter x2, local copies, waits for them, and re-layouts, pack_rows(): jnp.zeros((buffer_rows,) + rows.shape[1:], rows.dtype).at[target]  11.1 us
    all_to_all x1, waiting for transfers between devices, shards(): lax.all_to_all(upstream_send, 'adapter', split_axis=0, concat_axis=0, til...  10.7 us
    psum x1, blocking collectives, shards(): low_all = lax.psum(low_all, 'tensor')  9.6 us
    gather x1, local copies, waits for them, and re-layouts, shards(): lax.all_to_all(token_input_rows, 'adapter', split_axis=0, concat_axis=0,...  8.85 us
  transfers between devices with their start and end apart: 7, of which 6 were waited for; matrix products, arithmetic and copies ran while one was open for 13% of the time, Pallas kernels for 0%

commit v1 on v0

v1 whole, which is shorter than its diff:
```python
import jax
import jax.numpy as jnp
from jax import lax
from jax.experimental import pallas as pl
from jax.experimental.pallas import tpu as pltpu
from jax.sharding import PartitionSpec as P

MESH = pl.DeviceIdType.MESH
F32 = jnp.float32
BF16 = jnp.bfloat16
SCALE = 2.0
CHUNKS = 8
SMALL_CHUNKS = 2


def dot(a, b):
    return lax.dot_general(a, b, (((1,), (0,)), ((), ())), preferred_element_type=F32)


def dot_nt(a, b):
    return lax.dot_general(a, b, (((1,), (1,)), ((), ())), preferred_element_type=F32)


def tiled(total, tile, body):
    tile = min(tile, total)

    def step(i, carry):
        body(pl.ds(pl.multiple_of(i * tile, tile), tile))
        return carry

    lax.fori_loop(0, total // tile, step, 0)


def make_kernel(n, nx, nc, ranks, slots, planes):
    def kernel(
        ta_ref, asr_ref, tok_ref, w_hbm, a_ref, b_ref, u_ref,
        proj_ref, dxo_ref, gd_ref, gu_ref,
        w_ref, ta2, tok2, u2, ufull, basep, baser, fb,
        pack_m, mask_h, mask_r, spread_s, spread_t,
        send_t, recv_t, send_u, recv_u, ret_t, back_t, ret_u, back_u,
        rb_hot, rl_hot, rr,
        b_r, b_l, b_sr, b_sl, bh,
        c_r, c_l, c_sr, c_sl, g_hot, ah,
        v_r, v_l, v_sr, v_sl, gv_hot,
        dx2, dxs, lo2, los,
        wsem, lsem, sib_s, sib_r, ux_s, ux_r, bs_s, bs_r, rk_s, rk_r, aa_s, aa_r,
        bc_s, bc_r, cc_s, cc_r, vc_s, vc_r,
    ):
        td, d = tok_ref.shape
        er = a_ref.shape[0]
        e_local = er // ranks
        vl = u_ref.shape[1]
        v = w_ref.shape[1]
        dh, vh = d // nc, vl // nc
        t2 = nc * td
        ns = n * slots
        z, x, c = lax.axis_index("adapter"), lax.axis_index("tensor"), lax.axis_index("dp")
        sib = lax.rem(c + 1, nc)
        me_xc = x * nc + c
        my_cols = pl.ds(pl.multiple_of(c * dh, dh), dh)
        sib_cols = pl.ds(pl.multiple_of(sib * dh, dh), dh)
        my_vcols = pl.ds(pl.multiple_of(c * vh, vh), vh)
        sib_vcols = pl.ds(pl.multiple_of(sib * vh, vh), vh)
        my_rows = pl.ds(pl.multiple_of(c * td, td), td)
        sib_rows = pl.ds(pl.multiple_of(sib * td, td), td)

        w_copy = pltpu.make_async_copy(w_hbm, w_ref, wsem)
        w_copy.start()

        xc_peers = []
        for j in range(1, nx * nc):
            o = lax.rem(me_xc + j, nx * nc)
            xc_peers.append((o, o // nc, o % nc))
        z_peers = [lax.rem(z + j, n) for j in range(1, n)]
        x_peers = [lax.rem(x + j, nx) for j in range(1, nx)]

        barrier = pltpu.get_barrier_semaphore()
        for _, px, pc in xc_peers:
            pl.semaphore_signal(barrier, inc=1, device_id={"tensor": px, "dp": pc}, device_id_type=MESH)
        for pz in z_peers:
            pl.semaphore_signal(barrier, inc=1, device_id={"adapter": pz}, device_id_type=MESH)
        pl.semaphore_wait(barrier, len(xc_peers) + len(z_peers))

        def sib_copy(k, src, dst):
            return pltpu.make_async_remote_copy(
                src, dst, sib_s.at[k], sib_r.at[k], device_id={"dp": sib}, device_id_type=MESH
            )

        def z_copy(k, src, dst, to, frm):
            return pltpu.make_async_remote_copy(
                src, dst, aa_s.at[k, to], aa_r.at[k, frm], device_id={"adapter": to}, device_id_type=MESH
            )

        ta_c = sib_copy(0, ta_ref, ta2.at[c])
        tok_c = sib_copy(1, tok_ref.at[:, sib_cols], tok2.at[my_rows])
        u_c = sib_copy(2, u_ref.at[:, sib_vcols], u2.at[my_rows])
        ta_c.start()
        u_c.start()
        tok_c.start()
        for px in x_peers:
            pltpu.make_async_remote_copy(
                u_ref, ufull.at[x], ux_s.at[px], ux_r.at[x], device_id={"tensor": px}, device_id_type=MESH
            ).start()
        tok_l = pltpu.make_async_copy(tok_ref.at[:, my_cols], tok2.at[my_rows_of(c, td)], lsem.at[0])
        u_l = pltpu.make_async_copy(u_ref.at[:, my_vcols], u2.at[my_rows_of(c, td)], lsem.at[1])
        tok_l.start()
        u_l.start()
        ta2[c] = ta_ref[...]
        ufull[x] = u_ref[...]

        ta_c.wait_recv()
        ids = jnp.concatenate([ta2[i] for i in range(nc)], axis=1)
        at = asr_ref.shape[1]
        match = (lax.broadcasted_iota(jnp.int32, (at, t2), 0) == ids).astype(F32).astype(BF16)
        table = jnp.broadcast_to(asr_ref[...].astype(F32), (8, at)).astype(BF16)
        storage = dot(table, match)[0:1, :]
        owner = jnp.floor(storage * (1.0 / e_local))
        slot = storage - owner * e_local
        n8 = max(8, n)
        own_iota = lax.broadcasted_iota(jnp.int32, (n8, t2), 0).astype(F32)
        own_hit = jnp.where(own_iota == owner, 1.0, 0.0)
        loads = jnp.sum(own_hit, axis=1, keepdims=True)
        top = jnp.max(loads)
        hot = jnp.sum(jnp.where(loads == top, lax.broadcasted_iota(jnp.int32, (n8, 1), 0).astype(F32), 0.0))
        zf = z.astype(F32)
        w_is = jnp.where(hot == zf, 1.0, 0.0)
        w_lt = jnp.where(hot < zf, 1.0, 0.0)
        w_gt = jnp.where(hot > zf, 1.0, 0.0)
        tri = (
            lax.broadcasted_iota(jnp.int32, (t2, t2), 0) < lax.broadcasted_iota(jnp.int32, (t2, t2), 1)
        ).astype(F32).astype(BF16)
        pos = jnp.sum(dot(own_hit.astype(BF16), tri) * own_hit, axis=0, keepdims=True)
        target = jnp.where(owner == hot, -1.0, owner * slots + pos)
        pack_m[...] = jnp.where(
            lax.broadcasted_iota(jnp.int32, (ns, t2), 0).astype(F32) == target, 1.0, 0.0
        ).astype(BF16)
        begin = jnp.where(owner == hot, slot * ranks, -1.0 * ranks)
        er_iota = lax.broadcasted_iota(jnp.int32, (er, t2), 0).astype(F32)
        mask_h[...] = jnp.where(er_iota >= begin, 1.0, 0.0) * jnp.where(er_iota < begin + ranks, 1.0, 0.0)
        slot_hit = jnp.where(
            lax.broadcasted_iota(jnp.int32, (128, t2), 0).astype(F32) == slot, 1.0, 0.0
        ).astype(BF16)

        def clear_edges(right, left):
            @pl.when(z == 0)
            def _():
                right[...] = jnp.zeros_like(right)

            @pl.when(z == n - 1)
            def _():
                left[...] = jnp.zeros_like(left)

        def load(ref, rows):
            total = ref[0, rows, :].astype(F32)
            for p in range(1, planes):
                total += ref[p, rows, :].astype(F32)
            return total

        def store(ref, rows, value):
            for p in range(planes):
                part = value.astype(BF16)
                ref[p, rows, :] = part
                value = value - part.astype(F32)

        def chain_copy(src, dst, ssem, rsem, way, k, rows, to):
            return [
                pltpu.make_async_remote_copy(
                    src.at[p, rows], dst.at[p, rows], ssem.at[way, p, k], rsem.at[way, p, k],
                    device_id={"adapter": to}, device_id_type=MESH,
                )
                for p in range(planes)
            ]

        def chain_step(s, chunks, rr_, rl_, sr_, sl_, ssem, rsem, value):
            rc = er // chunks
            for way, (rin, sout, lag, edge_in, edge_out, step) in enumerate((
                (rr_, sr_, z, z == 0, z == n - 1, 1),
                (rl_, sl_, n - 1 - z, z == n - 1, z == 0, -1),
            )):
                k = s - lag

                @pl.when(jnp.logical_and(k >= 0, k < chunks))
                def _():
                    rows = pl.ds(pl.multiple_of(k * rc, rc), rc)
                    to = lax.rem(z + step + n, n)

                    @pl.when(jnp.logical_not(edge_in))
                    def _():
                        for cp in chain_copy(sout, rin, ssem, rsem, way, k, rows, to):
                            cp.wait_recv()

                    @pl.when(jnp.logical_not(edge_out))
                    def _():
                        store(sout, rows, value(way, rows, load(rin, rows)))
                        for cp in chain_copy(sout, rin, ssem, rsem, way, k, rows, to):
                            cp.start()

        def chain_finish(chunks, rr_, rl_, sr_, sl_, ssem, rsem):
            rc = er // chunks
            for way, (rin, sout, edge_out, step) in enumerate(
                ((rr_, sr_, z == n - 1, 1), (rl_, sl_, z == 0, -1))
            ):
                to = lax.rem(z + step + n, n)

                @pl.when(jnp.logical_not(edge_out))
                def _():
                    for k in range(chunks):
                        for cp in chain_copy(sout, rin, ssem, rsem, way, k, pl.ds(k * rc, rc), to):
                            cp.wait_send()

        clear_edges(b_r, b_l)
        clear_edges(c_r, c_l)
        clear_edges(v_r, v_l)

        b_args = (SMALL_CHUNKS, b_r, b_l, b_sr, b_sl, bc_s, bc_r)

        def b_value(way, rows, got):
            return w_is * b_ref[rows, my_vcols].astype(F32) + (1.0 - w_is) * got

        b_steps = SMALL_CHUNKS + n - 1
        chain_step(0, *b_args, b_value)
        tok_l.wait()
        u_l.wait()
        u_c.wait_recv()
        send_u[:, 0:vh] = dot(pack_m[...], u2[...]).astype(BF16)
        send_u[:, vh : vh + 128] = dot_nt(pack_m[...], slot_hit).astype(BF16)
        for pz in z_peers:
            z_copy(
                1, send_u.at[pl.ds(pl.multiple_of(pz * slots, slots), slots)],
                recv_u.at[pl.ds(pl.multiple_of(z * slots, slots), slots)], pz, z,
            ).start()
        chain_step(1, *b_args, b_value)
        tok_c.wait_recv()

        def pack_tile(cols):
            send_t[:, cols] = dot(pack_m[...], tok2[:, cols]).astype(BF16)

        tiled(dh, 512, pack_tile)
        my_slots = pl.ds(pl.multiple_of(z * slots, slots), slots)
        for pz in z_peers:
            z_copy(
                0, send_t.at[pl.ds(pl.multiple_of(pz * slots, slots), slots)], recv_t.at[my_slots], pz, z
            ).start()
        recv_t[my_slots, :] = send_t[my_slots, :]
        recv_u[my_slots, :] = send_u[my_slots, :]
        for s in range(2, b_steps):
            chain_step(s, *b_args, b_value)
        rows_all = pl.ds(0, er)
        bh[...] = (
            w_is * b_ref[:, my_vcols].astype(F32) + w_lt * load(b_r, rows_all) + w_gt * load(b_l, rows_all)
        ).astype(BF16)

        def rank_send(rnd, ref):
            for _, px, pc in xc_peers:
                pltpu.make_async_remote_copy(
                    ref.at[me_xc], ref.at[me_xc], rk_s.at[rnd, px * nc + pc], rk_r.at[rnd, me_xc],
                    device_id={"tensor": px, "dp": pc}, device_id_type=MESH,
                ).start()

        def rank_sum(rnd, ref):
            for o, px, pc in xc_peers:
                cp = pltpu.make_async_remote_copy(
                    ref.at[me_xc], ref.at[o], rk_s.at[rnd, o], rk_r.at[rnd, o],
                    device_id={"tensor": px, "dp": pc}, device_id_type=MESH,
                )
                cp.wait_recv()
                cp.wait_send()
            total = ref[0]
            for i in range(1, nx * nc):
                total += ref[i]
            return total

        def fold(full):
            return jnp.sum(full.reshape(e_local, ranks, full.shape[1]), axis=0)

        def spread(rank_rows, mask):
            rounded = rank_rows.astype(BF16).astype(F32)
            return jnp.concatenate([rounded] * e_local, axis=0) * mask

        rb_hot[me_xc] = fold(dot_nt(bh[...], u2[...]) * mask_h[...])
        rank_send(0, rb_hot)

        w_copy.wait()

        def base_tile(cols):
            basep[:, cols] = dot(tok_ref[...], w_ref[:, cols])

        tiled(v, 256, base_tile)
        for px in x_peers:
            pltpu.make_async_remote_copy(
                basep.at[:, pl.ds(pl.multiple_of(px * vl, vl), vl)], baser.at[x], bs_s.at[px], bs_r.at[x],
                device_id={"tensor": px}, device_id_type=MESH,
            ).start()

        s_back = spread(rank_sum(0, rb_hot), mask_h[...])
        spread_s[...] = s_back.astype(BF16)
        spread_t[...] = s_back.T.astype(BF16)

        def g_tile(cols):
            g_hot[:, cols] = SCALE * dot(spread_s[...], tok2[:, cols])

        tiled(dh, 512, g_tile)

        def c_value(way, rows, got):
            add = w_gt if way == 0 else w_lt
            return w_is * a_ref[rows, my_cols].astype(F32) + (1.0 - w_is) * got + add * g_hot[rows, :]

        c_args = (CHUNKS, c_r, c_l, c_sr, c_sl, cc_s, cc_r)

        def frozen_back():
            for px in x_peers:
                cp = pltpu.make_async_remote_copy(
                    u_ref, ufull.at[px], ux_s.at[px], ux_r.at[px], device_id={"tensor": px}, device_id_type=MESH
                )
                cp.wait_recv()
                cp.wait_send()
            up = jnp.concatenate([ufull[i] for i in range(nx)], axis=1)

            def tile(cols):
                fb[:, cols] = dot_nt(up, w_ref[cols, :])

            tiled(d, 512, tile)

        def rank_received():
            for pz in z_peers:
                ps = pl.ds(pl.multiple_of(pz * slots, slots), slots)
                for k, (src, dst) in enumerate(((send_t, recv_t), (send_u, recv_u))):
                    cp = z_copy(k, src.at[ps], dst.at[ps], pz, pz)
                    cp.wait_recv()
                    cp.wait_send()
            e_iota = lax.broadcasted_iota(jnp.int32, (er, 128), 0)
            j_iota = lax.broadcasted_iota(jnp.int32, (er, 128), 1) * ranks
            pick = jnp.where(e_iota >= j_iota, 1.0, 0.0) * jnp.where(e_iota < j_iota + ranks, 1.0, 0.0)
            mask_r[...] = dot_nt(pick.astype(BF16), recv_u[:, vh : vh + 128])
            rr[me_xc, 0:ranks, :] = fold(dot_nt(a_ref[:, my_cols], recv_t[...]) * mask_r[...])
            rr[me_xc, ranks : 2 * ranks, :] = fold(dot_nt(b_ref[:, my_vcols], recv_u[:, 0:vh]) * mask_r[...])
            rank_send(1, rr)

        def owner_work():
            both = rank_sum(1, rr)
            low = spread(both[0:ranks], mask_r[...])
            back = spread(both[ranks : 2 * ranks], mask_r[...])
            low_b, back_b = low.astype(BF16), back.astype(BF16)
            low_tr, back_tr = low.T.astype(BF16), back.T.astype(BF16)
            gu_ref[:, my_vcols] = SCALE * dot(low_b, recv_u[:, 0:vh])
            ret_u[...] = (SCALE * dot(low_tr, b_ref[:, my_vcols])).astype(BF16)
            for j in range(0, dh, 512):
                cols = pl.ds(j, 512)
                out_cols = pl.ds(pl.multiple_of(c * dh + j, 512), 512)
                gd_ref[:, out_cols] = SCALE * dot(back_b, recv_t[:, cols])
                ret_t[:, cols] = (SCALE * dot(back_tr, a_ref[:, out_cols])).astype(BF16)

        def send_returns():
            for pz in z_peers:
                ps = pl.ds(pl.multiple_of(pz * slots, slots), slots)
                z_copy(3, ret_u.at[ps], back_u.at[my_slots], pz, z).start()
                z_copy(2, ret_t.at[ps], back_t.at[my_slots], pz, z).start()
            back_t[my_slots, :] = ret_t[my_slots, :]
            back_u[my_slots, :] = ret_u[my_slots, :]

        c_steps = CHUNKS + n - 1
        hooks = {0: frozen_back, 4: rank_received, 6: owner_work, 7: send_returns}
        for s in range(c_steps):
            chain_step(s, *c_args, c_value)
            if s in hooks:
                hooks[s]()

        ah[...] = (
            w_is * a_ref[:, my_cols].astype(F32) + w_lt * load(c_r, rows_all) + w_gt * load(c_l, rows_all)
        ).astype(BF16)
        for j in range(0, t2, td):
            rl_hot[me_xc, :, j : j + td] = fold(dot_nt(ah[...], tok2[j : j + td, :]) * mask_h[:, j : j + td])
        rank_send(2, rl_hot)
        keep = 1.0 - w_is

        def gd_tile(i, carry):
            cols = pl.ds(pl.multiple_of(i * 512, 512), 512)
            out_cols = pl.ds(pl.multiple_of(c * dh + i * 512, 512), 512)
            total = g_hot[:, cols]
            for p in range(planes):
                total += c_r[p, :, cols].astype(F32) + c_l[p, :, cols].astype(F32)
            gd_ref[:, out_cols] = keep * gd_ref[:, out_cols] + w_is * total
            return carry

        lax.fori_loop(0, dh // 512, gd_tile, 0)
        gd_c = sib_copy(3, gd_ref.at[:, my_cols], gd_ref.at[:, my_cols])
        gd_c.start()

        low_s = spread(rank_sum(2, rl_hot), mask_h[...])
        low_b = low_s.astype(BF16)
        gv_hot[...] = SCALE * dot(low_b, u2[...])
        v_args = (SMALL_CHUNKS, v_r, v_l, v_sr, v_sl, vc_s, vc_r)

        def v_value(way, rows, got):
            return got + gv_hot[rows, :]

        chain_step(0, *v_args, v_value)

        def dx_tile(cols):
            dx2[:, cols] = (SCALE * dot(spread_t[...], ah[:, cols])).astype(BF16)

        tiled(dh, 512, dx_tile)
        chain_step(1, *v_args, v_value)
        lora_hot = (SCALE * dot(low_s.T.astype(BF16), bh[...])).astype(BF16).astype(F32)
        unpack = pack_m[...].astype(F32).T.astype(BF16)
        for s in range(2, SMALL_CHUNKS + n - 1):
            chain_step(s, *v_args, v_value)
        gu_ref[:, my_vcols] = keep * gu_ref[:, my_vcols] + w_is * (
            gv_hot[...] + load(v_r, rows_all) + load(v_l, rows_all)
        )
        gu_c = sib_copy(4, gu_ref.at[:, my_vcols], gu_ref.at[:, my_vcols])
        gu_c.start()

        for pz in z_peers:
            ps = pl.ds(pl.multiple_of(pz * slots, slots), slots)
            cp = z_copy(3, ret_u.at[ps], back_u.at[ps], pz, pz)
            cp.wait_recv()
            cp.wait_send()
        lo2[...] = (lora_hot + dot(unpack, back_u[...])).astype(BF16)
        lo_c = sib_copy(5, lo2.at[sib_rows], los)
        lo_c.start()
        for pz in z_peers:
            ps = pl.ds(pl.multiple_of(pz * slots, slots), slots)
            cp = z_copy(2, ret_t.at[ps], back_t.at[ps], pz, pz)
            cp.wait_recv()
            cp.wait_send()

        def un_tile(cols):
            dx2[:, cols] = (dx2[:, cols].astype(F32) + dot(unpack, back_t[:, cols])).astype(BF16)

        tiled(dh, 512, un_tile)
        dx_c = sib_copy(6, dx2.at[sib_rows], dxs)
        dx_c.start()

        for px in x_peers:
            cp = pltpu.make_async_remote_copy(
                basep.at[:, pl.ds(pl.multiple_of(px * vl, vl), vl)], baser.at[px], bs_s.at[px], bs_r.at[px],
                device_id={"tensor": px}, device_id_type=MESH,
            )
            cp.wait_recv()
            cp.wait_send()
        x_cols = pl.ds(pl.multiple_of(x * vl, vl), vl)
        baser[x] = basep[:, x_cols]
        frozen = baser[0]
        for i in range(1, nx):
            frozen += baser[i]
        basep[:, 0:vl] = frozen
        proj_ref[:, my_vcols] = (basep[:, my_vcols] + lo2[my_rows, :].astype(F32)).astype(BF16)
        dxo_ref[:, my_cols] = (fb[:, my_cols] + dx2[my_rows, :].astype(F32)).astype(BF16)
        lo_c.wait()
        proj_ref[:, sib_vcols] = (basep[:, sib_vcols] + los[...].astype(F32)).astype(BF16)
        dx_c.wait()
        dxo_ref[:, sib_cols] = (fb[:, sib_cols] + dxs[...].astype(F32)).astype(BF16)
        sib_copy(3, gd_ref.at[:, my_cols], gd_ref.at[:, sib_cols]).wait()
        sib_copy(4, gu_ref.at[:, my_vcols], gu_ref.at[:, sib_vcols]).wait()
        ta_c.wait_send()
        tok_c.wait_send()
        u_c.wait_send()
        chain_finish(*b_args)
        chain_finish(*c_args)
        chain_finish(*v_args)

    return kernel


def my_rows_of(c, td):
    return pl.ds(pl.multiple_of(c * td, td), td)


def shards(tokens, weight, down, up, token_adapter, storage_row, upstream):
    n, nx, nc = lax.axis_size("adapter"), lax.axis_size("tensor"), lax.axis_size("dp")
    td, d = tokens.shape
    e_local, ranks, vl = up.shape
    er, v = e_local * ranks, weight.shape[1]
    hot_load = 3 * td // n
    most = -(-(td - hot_load) // (n - 1))
    slots = -(-(nc * most) // 16) * 16
    planes = 1 if n <= 4 else 2
    dh, vh, t2, ns, xc = d // nc, vl // nc, nc * td, n * slots, nx * nc
    vm = pltpu.VMEM
    dma = pltpu.SemaphoreType.DMA
    scratch = [
        vm((d, v), BF16), vm((nc, 1, td), jnp.int32), vm((t2, dh), BF16), vm((t2, vh), BF16),
        vm((nx, td, vl), BF16), vm((td, v), F32), vm((nx, td, vl), F32), vm((td, d), F32),
        vm((ns, t2), BF16), vm((er, t2), F32), vm((er, ns), F32), vm((er, t2), BF16), vm((t2, er), BF16),
        vm((ns, dh), BF16), vm((ns, dh), BF16), vm((ns, vh + 128), BF16), vm((ns, vh + 128), BF16),
        vm((ns, dh), BF16), vm((ns, dh), BF16), vm((ns, vh), BF16), vm((ns, vh), BF16),
        vm((xc, ranks, t2), F32), vm((xc, ranks, t2), F32), vm((xc, 2 * ranks, ns), F32),
        *[vm((planes, er, vh), BF16)] * 4, vm((er, vh), BF16),
        *[vm((planes, er, dh), BF16)] * 4, vm((er, dh), F32), vm((er, dh), BF16),
        *[vm((planes, er, vh), BF16)] * 4, vm((er, vh), F32),
        vm((t2, dh), BF16), vm((td, dh), BF16), vm((t2, vh), BF16), vm((td, vh), BF16),
        dma, dma((2,)), dma((7,)), dma((7,)), dma((nx,)), dma((nx,)), dma((nx,)), dma((nx,)),
        dma((3, xc)), dma((3, xc)), dma((4, n)), dma((4, n)),
        dma((2, planes, SMALL_CHUNKS)), dma((2, planes, SMALL_CHUNKS)),
        dma((2, planes, CHUNKS)), dma((2, planes, CHUNKS)),
        dma((2, planes, SMALL_CHUNKS)), dma((2, planes, SMALL_CHUNKS)),
    ]
    vspec = pl.BlockSpec(memory_space=pltpu.VMEM)
    proj, dx, gd, gu = pl.pallas_call(
        make_kernel(n, nx, nc, ranks, slots, planes),
        out_shape=(
            jax.ShapeDtypeStruct((td, vl), BF16),
            jax.ShapeDtypeStruct((td, d), BF16),
            jax.ShapeDtypeStruct((er, d), F32),
            jax.ShapeDtypeStruct((er, vl), F32),
        ),
        in_specs=[vspec, vspec, vspec, pl.BlockSpec(memory_space=pl.ANY), vspec, vspec, vspec],
        out_specs=(vspec,) * 4,
        scratch_shapes=scratch,
        compiler_params=pltpu.CompilerParams(
            collective_id=0, has_side_effects=True, vmem_limit_bytes=60 * 1024 * 1024
        ),
        cost_estimate=pl.CostEstimate(flops=8_000_000_000, bytes_accessed=20_000_000, transcendentals=0),
    )(
        token_adapter.reshape(1, td), storage_row.reshape(1, -1), tokens, weight,
        down.reshape(er, d), up.reshape(er, vl), upstream,
    )
    return proj, dx, gd.reshape(e_local, ranks, d), gu.reshape(e_local, ranks, vl)


def solution(mesh):
    return jax.shard_map(
        shards,
        mesh=mesh,
        in_specs=(
            P(("groups", "adapter", "dp"), "tensor"),
            P("tensor", None),
            P(("groups", "adapter"), None, "tensor"),
            P(("groups", "adapter"), None, "tensor"),
            P(("groups", "adapter", "dp")),
            P("groups"),
            P(("groups", "adapter", "dp"), "tensor"),
        ),
        out_specs=(
            P(("groups", "adapter", "dp"), "tensor"),
            P(("groups", "adapter", "dp"), "tensor"),
            P(("groups", "adapter"), None, "tensor"),
            P(("groups", "adapter"), None, "tensor"),
        ),
        check_vma=False,
    )
```

time: 398 us -> 134 us (0.34)
  waiting for transfers between devices: 264 us -> 0 us
  Pallas kernels: 0 us -> 126 us
  matrix products: 34.7 us -> 0 us
  blocking collectives: 24.2 us -> 0 us
  starting transfers between devices: 24.2 us -> 0 us
  local copies, waits for them, and re-layouts: 30 us -> 7.76 us
  between operations: 15.6 us -> 0.64 us
  other arithmetic: 4.19 us -> 0 us
    all_to_all x5 -> x0, waiting for transfers between devices: 263 us -> none  [the longest x1 137 us: shards(): lax.all_to_all(feature_send, 'adapter', split_axis=0, concat_axis=0, tile...]
    pallas_call x0 -> x1, Pallas kernels: none -> 126 us  [shards(): pl.pallas_call(make_kernel(n, nx, nc, ranks, slots, planes), out_shape=(j...]
    dot_general x8 -> x0, matrix products: 34.7 us -> none  [the longest x1 7.67 us: shards(): lax.dot_general(lax.all_gather(upstream, 'tensor', axis=1, tiled=True), f...]
    all_to_all x5 -> x0, starting transfers between devices: 24.1 us -> none  [the longest x1 6.32 us: shards(): lax.all_to_all(slot_send, 'adapter', split_axis=0, concat_axis=0, tiled=T...]
    all_gather x1 -> x0, blocking collectives: 14.6 us -> none  [shards(): lax.all_gather(upstream, 'tensor', axis=1, tiled=True)]
    scatter x3 -> x0, local copies, waits for them, and re-layouts: 12.5 us -> none  [the longest x2 11.1 us: pack_rows(): jnp.zeros((buffer_rows,) + rows.shape[1:], rows.dtype).at[target]]
    gather x2 -> x0, local copies, waits for them, and re-layouts: 10 us -> none  [the longest x1 8.85 us: shards(): lax.all_to_all(token_input_rows, 'adapter', split_axis=0, concat_axis=0,...]
    psum x1 -> x0, blocking collectives: 9.6 us -> none  [shards(): low_all = lax.psum(low_all, 'tensor')]
  transfers between devices with their start and end apart: 7 -> 0, of which waited for: 6 -> 0; matrix products, arithmetic and copies ran while one was open for 13% -> 0% of each run, Pallas kernels for 0% -> 0%
where the time goes in v1:
time: 134 us
  Pallas kernels  126 us (94%)
  local copies, waits for them, and re-layouts  7.76 us (6%)
    pallas_call x1, Pallas kernels, shards(): pl.pallas_call(make_kernel(n, nx, nc, ranks, slots, planes), out_shape=(j...  126 us
    unnamed x8, local copies, waits for them, and re-layouts  7.76 us

profile of v1, /device:TPU:0, one launch (start us, length us, event | category | flops | bytes accessed | tf_op | source)
XLA Modules:
  0.0 134.2 jit_solution(1505389086833386468)
XLA Ops:
  0.6 125.8 %shard_map.102 = (bf16[256,512]{1,0:T(8,128)(2,1)}, bf16[256,4096]{1,0:T(8,128)(2,1)}, f32[256,4096]{1,0:T(8,128)}, f32[256,512]{1,0:T(8,128)}) custom-call(s32[1,256]{1,0:T(1,128)} %bitcast.10, s32[1,64]{1,0:T(1,128)} %bitcast.11, bf16[256,4096]{1,0:T(8,128)(2,1)} %tok_ref.1, bf16[4096,1024]{1,0:T(8,128)(2,1)} %w_hbm.1, bf16[256,4096]{1,0:T(8,128)(2,1)} %bitcast.8, ...), custom_call_target="tpu_custom_call" | custom-call | flops 8000000000 | bytes 20000000 | tf_op jit(solution)/shard_map/pallas_call | solution.py:500
  126.4 1.7 %copy.15 = bf16[256,512]{1,0:T(8,128)(2,1)} copy(bf16[256,512]{1,0:T(8,128)(2,1)} %get-tuple-element.16) | data formatting | bytes 524288
  128.1 0.0 copy-start
  128.1 3.3 %copy.16 = bf16[256,4096]{1,0:T(8,128)(2,1)} copy(bf16[256,4096]{1,0:T(8,128)(2,1)} %get-tuple-element.17) | data formatting | bytes 4194304
  131.3 0.0 copy-done
  131.3 0.0 copy-start.1
  131.3 2.0 %copy.17 = f32[16,16,4096]{2,1,0:T(8,128)} copy(f32[16,16,4096]{2,1,0:T(8,128)S(1)} %bitcast.6) | data formatting | bytes 8388608
  133.4 0.0 copy-done.1
  133.4 0.8 copy.18
Async XLA Ops:
  128.1 3.3 %copy-start = (f32[256,4096]{1,0:T(8,128)S(1)}, f32[256,4096]{1,0:T(8,128)}, u32[]{:S(2)}) copy-start(f32[256,4096]{1,0:T(8,128)} %get-tuple-element.10) | copy-start | bytes 12582916
  131.3 2.0 %copy-start.1 = (f32[256,512]{1,0:T(8,128)S(1)}, f32[256,512]{1,0:T(8,128)}, u32[]{:S(2)}) copy-start(f32[256,512]{1,0:T(8,128)} %get-tuple-element.11) | copy-start | bytes 1572868

commit v2 on v1

--- a/solution.py
+++ b/solution.py
@@ -10,7 +10,7 @@
 BF16 = jnp.bfloat16
 SCALE = 2.0
 CHUNKS = 8
-SMALL_CHUNKS = 2
+LAG = 2
 
 
 def dot(a, b):
@@ -39,12 +39,12 @@
         pack_m, mask_h, mask_r, spread_s, spread_t,
         send_t, recv_t, send_u, recv_u, ret_t, back_t, ret_u, back_u,
         rb_hot, rl_hot, rr,
-        b_r, b_l, b_sr, b_sl, bh,
+        ball, bh,
         c_r, c_l, c_sr, c_sl, g_hot, ah,
         v_r, v_l, v_sr, v_sl, gv_hot,
         dx2, dxs, lo2, los,
         wsem, lsem, sib_s, sib_r, ux_s, ux_r, bs_s, bs_r, rk_s, rk_r, aa_s, aa_r,
-        bc_s, bc_r, cc_s, cc_r, vc_s, vc_r,
+        cc_s, cc_r, vc_s, vc_r,
     ):
         td, d = tok_ref.shape
         er = a_ref.shape[0]
@@ -94,6 +94,9 @@
         ta_c = sib_copy(0, ta_ref, ta2.at[c])
         tok_c = sib_copy(1, tok_ref.at[:, sib_cols], tok2.at[my_rows])
         u_c = sib_copy(2, u_ref.at[:, sib_vcols], u2.at[my_rows])
+        for pz in z_peers:
+            z_copy(4, b_ref.at[:, my_vcols], ball.at[z], pz, z).start()
+        ball[z] = b_ref[:, my_vcols]
         ta_c.start()
         u_c.start()
         tok_c.start()
@@ -171,11 +174,11 @@
                 for p in range(planes)
             ]
 
-        def chain_step(s, chunks, rr_, rl_, sr_, sl_, ssem, rsem, value):
+        def chain_step(s, chunks, lag_by, rr_, rl_, sr_, sl_, ssem, rsem, value):
             rc = er // chunks
             for way, (rin, sout, lag, edge_in, edge_out, step) in enumerate((
-                (rr_, sr_, z, z == 0, z == n - 1, 1),
-                (rl_, sl_, n - 1 - z, z == n - 1, z == 0, -1),
+                (rr_, sr_, lag_by * z, z == 0, z == n - 1, 1),
+                (rl_, sl_, lag_by * (n - 1 - z), z == n - 1, z == 0, -1),
             )):
                 k = s - lag
 
@@ -195,7 +198,7 @@
                         for cp in chain_copy(sout, rin, ssem, rsem, way, k, rows, to):
                             cp.start()
 
-        def chain_finish(chunks, rr_, rl_, sr_, sl_, ssem, rsem):
+        def chain_finish(chunks, lag_by, rr_, rl_, sr_, sl_, ssem, rsem):
             rc = er // chunks
             for way, (rin, sout, edge_out, step) in enumerate(
                 ((rr_, sr_, z == n - 1, 1), (rl_, sl_, z == 0, -1))
@@ -208,17 +211,9 @@
                         for cp in chain_copy(sout, rin, ssem, rsem, way, k, pl.ds(k * rc, rc), to):
                             cp.wait_send()
 
-        clear_edges(b_r, b_l)
         clear_edges(c_r, c_l)
         clear_edges(v_r, v_l)
 
-        b_args = (SMALL_CHUNKS, b_r, b_l, b_sr, b_sl, bc_s, bc_r)
-
-        def b_value(way, rows, got):
-            return w_is * b_ref[rows, my_vcols].astype(F32) + (1.0 - w_is) * got
-
-        b_steps = SMALL_CHUNKS + n - 1
-        chain_step(0, *b_args, b_value)
         tok_l.wait()
         u_l.wait()
         u_c.wait_recv()
@@ -229,7 +224,6 @@
                 1, send_u.at[pl.ds(pl.multiple_of(pz * slots, slots), slots)],
                 recv_u.at[pl.ds(pl.multiple_of(z * slots, slots), slots)], pz, z,
             ).start()
-        chain_step(1, *b_args, b_value)
         tok_c.wait_recv()
 
         def pack_tile(cols):
@@ -243,12 +237,15 @@
             ).start()
         recv_t[my_slots, :] = send_t[my_slots, :]
         recv_u[my_slots, :] = send_u[my_slots, :]
-        for s in range(2, b_steps):
-            chain_step(s, *b_args, b_value)
+        for pz in z_peers:
+            cp = z_copy(4, b_ref.at[:, my_vcols], ball.at[pz], pz, pz)
+            cp.wait_recv()
+            cp.wait_send()
         rows_all = pl.ds(0, er)
-        bh[...] = (
-            w_is * b_ref[:, my_vcols].astype(F32) + w_lt * load(b_r, rows_all) + w_gt * load(b_l, rows_all)
-        ).astype(BF16)
+        hot_up = jnp.zeros((er, vh), F32)
+        for i in range(n):
+            hot_up += jnp.where(hot == i, 1.0, 0.0) * ball[i].astype(F32)
+        bh[...] = hot_up.astype(BF16)
 
         def rank_send(rnd, ref):
             for _, px, pc in xc_peers:
@@ -305,7 +302,7 @@
             add = w_gt if way == 0 else w_lt
             return w_is * a_ref[rows, my_cols].astype(F32) + (1.0 - w_is) * got + add * g_hot[rows, :]
 
-        c_args = (CHUNKS, c_r, c_l, c_sr, c_sl, cc_s, cc_r)
+        c_args = (CHUNKS, LAG, c_r, c_l, c_sr, c_sl, cc_s, cc_r)
 
         def frozen_back():
             for px in x_peers:
@@ -358,8 +355,8 @@
             back_t[my_slots, :] = ret_t[my_slots, :]
             back_u[my_slots, :] = ret_u[my_slots, :]
 
-        c_steps = CHUNKS + n - 1
-        hooks = {0: frozen_back, 4: rank_received, 6: owner_work, 7: send_returns}
+        c_steps = CHUNKS + LAG * (n - 1)
+        hooks = {0: frozen_back, 7: rank_received, 10: owner_work, 13: send_returns}
         for s in range(c_steps):
             chain_step(s, *c_args, c_value)
             if s in hooks:
@@ -389,7 +386,7 @@
         low_s = spread(rank_sum(2, rl_hot), mask_h[...])
         low_b = low_s.astype(BF16)
         gv_hot[...] = SCALE * dot(low_b, u2[...])
-        v_args = (SMALL_CHUNKS, v_r, v_l, v_sr, v_sl, vc_s, vc_r)
+        v_args = (1, 1, v_r, v_l, v_sr, v_sl, vc_s, vc_r)
 
         def v_value(way, rows, got):
             return got + gv_hot[rows, :]
@@ -403,14 +400,6 @@
         chain_step(1, *v_args, v_value)
         lora_hot = (SCALE * dot(low_s.T.astype(BF16), bh[...])).astype(BF16).astype(F32)
         unpack = pack_m[...].astype(F32).T.astype(BF16)
-        for s in range(2, SMALL_CHUNKS + n - 1):
-            chain_step(s, *v_args, v_value)
-        gu_ref[:, my_vcols] = keep * gu_ref[:, my_vcols] + w_is * (
-            gv_hot[...] + load(v_r, rows_all) + load(v_l, rows_all)
-        )
-        gu_c = sib_copy(4, gu_ref.at[:, my_vcols], gu_ref.at[:, my_vcols])
-        gu_c.start()
-
         for pz in z_peers:
             ps = pl.ds(pl.multiple_of(pz * slots, slots), slots)
             cp = z_copy(3, ret_u.at[ps], back_u.at[ps], pz, pz)
@@ -419,6 +408,7 @@
         lo2[...] = (lora_hot + dot(unpack, back_u[...])).astype(BF16)
         lo_c = sib_copy(5, lo2.at[sib_rows], los)
         lo_c.start()
+        chain_step(2, *v_args, v_value)
         for pz in z_peers:
             ps = pl.ds(pl.multiple_of(pz * slots, slots), slots)
             cp = z_copy(2, ret_t.at[ps], back_t.at[ps], pz, pz)
@@ -431,6 +421,13 @@
         tiled(dh, 512, un_tile)
         dx_c = sib_copy(6, dx2.at[sib_rows], dxs)
         dx_c.start()
+        for s in range(3, n):
+            chain_step(s, *v_args, v_value)
+        gu_ref[:, my_vcols] = keep * gu_ref[:, my_vcols] + w_is * (
+            gv_hot[...] + load(v_r, rows_all) + load(v_l, rows_all)
+        )
+        gu_c = sib_copy(4, gu_ref.at[:, my_vcols], gu_ref.at[:, my_vcols])
+        gu_c.start()
 
         for px in x_peers:
             cp = pltpu.make_async_remote_copy(
@@ -456,7 +453,6 @@
         ta_c.wait_send()
         tok_c.wait_send()
         u_c.wait_send()
-        chain_finish(*b_args)
         chain_finish(*c_args)
         chain_finish(*v_args)
 
@@ -486,15 +482,13 @@
         vm((ns, dh), BF16), vm((ns, dh), BF16), vm((ns, vh + 128), BF16), vm((ns, vh + 128), BF16),
         vm((ns, dh), BF16), vm((ns, dh), BF16), vm((ns, vh), BF16), vm((ns, vh), BF16),
         vm((xc, ranks, t2), F32), vm((xc, ranks, t2), F32), vm((xc, 2 * ranks, ns), F32),
-        *[vm((planes, er, vh), BF16)] * 4, vm((er, vh), BF16),
+        vm((n, er, vh), BF16), vm((er, vh), BF16),
         *[vm((planes, er, dh), BF16)] * 4, vm((er, dh), F32), vm((er, dh), BF16),
         *[vm((planes, er, vh), BF16)] * 4, vm((er, vh), F32),
         vm((t2, dh), BF16), vm((td, dh), BF16), vm((t2, vh), BF16), vm((td, vh), BF16),
         dma, dma((2,)), dma((7,)), dma((7,)), dma((nx,)), dma((nx,)), dma((nx,)), dma((nx,)),
-        dma((3, xc)), dma((3, xc)), dma((4, n)), dma((4, n)),
-        dma((2, planes, SMALL_CHUNKS)), dma((2, planes, SMALL_CHUNKS)),
-        dma((2, planes, CHUNKS)), dma((2, planes, CHUNKS)),
-        dma((2, planes, SMALL_CHUNKS)), dma((2, planes, SMALL_CHUNKS)),
+        dma((3, xc)), dma((3, xc)), dma((5, n)), dma((5, n)),
+        dma((2, planes, CHUNKS)), dma((2, planes, CHUNKS)), dma((2, planes, 1)), dma((2, planes, 1)),
     ]
     vspec = pl.BlockSpec(memory_space=pltpu.VMEM)
     proj, dx, gd, gu = pl.pallas_call(

time: 134 us -> 108 us (0.81)
  Pallas kernels: 126 us -> 99.8 us
    pallas_call x1, Pallas kernels: 126 us -> 99.8 us  [shards(): pl.pallas_call(make_kernel(n, nx, nc, ranks, slots, planes), out_shape=(j...]
where the time goes in v2:
time: 108 us
  Pallas kernels  99.8 us (92%)
  local copies, waits for them, and re-layouts  7.76 us (7%)
    pallas_call x1, Pallas kernels, shards(): pl.pallas_call(make_kernel(n, nx, nc, ranks, slots, planes), out_shape=(j...  99.8 us
    unnamed x8, local copies, waits for them, and re-layouts  7.76 us

profile of v2, /device:TPU:0, one launch (start us, length us, event | category | flops | bytes accessed | tf_op | source)
XLA Modules:
  0.0 108.2 jit_solution(4000276652526781406)
XLA Ops:
  0.6 99.8 %shard_map.102 = (bf16[256,512]{1,0:T(8,128)(2,1)}, bf16[256,4096]{1,0:T(8,128)(2,1)}, f32[256,4096]{1,0:T(8,128)}, f32[256,512]{1,0:T(8,128)}) custom-call(s32[1,256]{1,0:T(1,128)} %bitcast.10, s32[1,64]{1,0:T(1,128)} %bitcast.11, bf16[256,4096]{1,0:T(8,128)(2,1)} %tok_ref.1, bf16[4096,1024]{1,0:T(8,128)(2,1)} %w_hbm.1, bf16[256,4096]{1,0:T(8,128)(2,1)} %bitcast.8, ...), custom_call_target="tpu_custom_call" | custom-call | flops 8000000000 | bytes 20000000 | tf_op jit(solution)/shard_map/pallas_call | solution.py:494
  100.5 1.7 %copy.15 = bf16[256,512]{1,0:T(8,128)(2,1)} copy(bf16[256,512]{1,0:T(8,128)(2,1)} %get-tuple-element.16) | data formatting | bytes 524288
  102.2 0.0 copy-start
  102.2 3.3 %copy.16 = bf16[256,4096]{1,0:T(8,128)(2,1)} copy(bf16[256,4096]{1,0:T(8,128)(2,1)} %get-tuple-element.17) | data formatting | bytes 4194304
  105.4 0.0 copy-done
  105.4 0.0 copy-start.1
  105.4 2.0 %copy.17 = f32[16,16,4096]{2,1,0:T(8,128)} copy(f32[16,16,4096]{2,1,0:T(8,128)S(1)} %bitcast.6) | data formatting | bytes 8388608
  107.5 0.0 copy-done.1
  107.5 0.8 copy.18
Async XLA Ops:
  102.2 3.3 %copy-start = (f32[256,4096]{1,0:T(8,128)S(1)}, f32[256,4096]{1,0:T(8,128)}, u32[]{:S(2)}) copy-start(f32[256,4096]{1,0:T(8,128)} %get-tuple-element.10) | copy-start | bytes 12582916
  105.4 2.0 %copy-start.1 = (f32[256,512]{1,0:T(8,128)S(1)}, f32[256,512]{1,0:T(8,128)}, u32[]{:S(2)}) copy-start(f32[256,512]{1,0:T(8,128)} %get-tuple-element.11) | copy-start | bytes 1572868
